TPU v7x, 256 devices: a whole 4x4x8 slice. The times are simulated.
256 devices in a mesh: tm: 8 (over x, y_lo), space: 32 (over z, y_hi, core).
Axes of the slice: x: 4, y: 4 (y_hi: 2, y_lo: 2; y = y_hi * 2 + y_lo), z: 8, core: 2. Of those that a mesh axis runs over, the one named last changes fastest.
Arguments:
- snapshots: bfloat16 [128, 256, 32768], P('tm', None, 'space'), may hold values from -6 to 6
- weights: float32 [32768], P('space'), may hold values from 1.5258789e-05 to 0.00024414062
Outputs:
- spectra: float32 [128, 128, 2, 128], P('space', 'tm')
All inputs are finite; a program needn't handle non-finite values.
Results may differ from a plain program's by a relative error of at most 0.0027.
Values may be sent and summed in bfloat16 or wider, within the bound.
No kernel may reach another device: no remote copies, remote signals or barrier semaphores. Data moves between devices by JAX's collectives and lax.ppermute only.
A program may use at most 192 MiB of HBM per device.

v0:
```python
import math

import jax
import jax.numpy as jnp
from jax import lax
from jax.sharding import PartitionSpec as P


def make_table(length, count):
    steps_t = jnp.arange(length, dtype=jnp.int32)
    freqs = jnp.arange(count, dtype=jnp.int32)
    phase = (freqs[:, None] * steps_t[None, :] % length).astype(jnp.float32) * (
        2.0 * math.pi / length
    )
    hann = 0.5 - 0.5 * jnp.cos(steps_t.astype(jnp.float32) * (2.0 * math.pi / length))
    factor = 1.0 / math.sqrt(3.0 * length / 8.0)
    table = jnp.concatenate([jnp.cos(phase), -jnp.sin(phase)], axis=0) * hann[None, :] * factor
    return table.astype(jnp.bfloat16)


def transform(block, point_weights):
    length = block.shape[1]
    count = length // 2
    table = make_table(length, count)
    coeffs = jnp.einsum("kt,btx->bkx", table, block, preferred_element_type=jnp.float32)
    coeffs = coeffs * jnp.sqrt(point_weights)[None, None, :]
    return coeffs.reshape(block.shape[0], 2, count, block.shape[2])


def cross_rows(coeffs):
    highest = lax.Precision.HIGHEST
    real_part = jnp.einsum("acfx,bcfx->afb", coeffs, coeffs, precision=highest)
    imag_part = jnp.einsum("afx,bfx->afb", coeffs[:, 0], coeffs[:, 1], precision=highest)
    imag_part = imag_part - jnp.einsum(
        "afx,bfx->afb", coeffs[:, 1], coeffs[:, 0], precision=highest
    )
    return jnp.stack([real_part, imag_part], axis=2)


def per_device(snapshots, weights):
    moved = lax.all_to_all(snapshots, "tm", split_axis=2, concat_axis=0, tiled=True)
    width = moved.shape[2]
    local_weights = lax.dynamic_slice_in_dim(weights, lax.axis_index("tm") * width, width, 0)
    coeffs = transform(moved, local_weights)
    partial_rows = lax.psum_scatter(cross_rows(coeffs), "space", scatter_dimension=0, tiled=True)
    spectra = lax.psum_scatter(partial_rows, "tm", scatter_dimension=1, tiled=True)
    return spectra


def solution(mesh):
    placed = (P("tm", None, "space"), P("space"))
    return jax.shard_map(
        per_device,
        mesh=mesh,
        in_specs=placed,
        out_specs=P("space", "tm", None, None),
        check_vma=False,
    )
```

profile of v0, /device:TPU:1, one launch (start us, length us, event | category | flops | bytes accessed | tf_op | source)
XLA Modules:
  0.0 616.3 jit_solution(8832547970531412455)
XLA Ops:
  6.5 12.6 %copy.9 = bf16[16,256,1024]{1,0,2:T(8,128)(2,1)} copy(bf16[16,256,1024]{2,1,0:T(8,128)(2,1)} %param.2) | data formatting | bytes 16777216 | tf_op args[0]
  19.1 5.9 all-to-all-start
  25.0 0.0 reduce-scatter.2.cloned.1.call-start
  25.0 0.8 dynamic-slice_sqrt_fusion
  25.8 0.5 sine_negate_fusion
  26.4 113.1 %all-to-all-done = bf16[16,256,1024]{1,0,2:T(8,128)(2,1)} async-done(((bf16[16,256,1024]{1,0,2:T(8,128)(2,1)}), bf16[16,256,1024]{1,0,2:T(8,128)(2,1)}, u32[]{:S(2)}, u32[]{:S(2)}) %all-to-all-start) | async-done | bytes 8388640 | tf_op jit(solution)/shard_map/all_to_all | solution.py:41
  139.5 12.8 %copy.10 = bf16[16,256,8,128]{3,1,0,2:T(8,128)(2,1)} copy(bf16[16,256,8,128]{1,0,3,2:T(8,128)(2,1)} %bitcast.1) | data formatting | bytes 16777216 | tf_op jit(solution)/shard_map/all_to_all | solution.py:41
  152.2 5.7 convolution_multiply_fusion
  158.0 0.0 copy-start
  158.0 5.7 copy-done
  163.7 6.4 %fusion.22 = (f32[128,1,128,128]{3,2,1,0:T(8,128)}, f32[128,1,128,128]{3,2,1,0:T(8,128)}) fusion(f32[128,2,128,128]{3,2,1,0:T(8,128)S(1)} %bitcast.35), kind=kLoop, calls=%fused_computation.32 | loop fusion | bytes 33554432 | tf_op jit(solution)/shard_map/slice | solution.py:33
  170.1 44.3 %fusion.4 = f32[128,128,1,128]{0,3,1,2:T(8,128)} fusion(f32[128,2,128,128]{3,2,1,0:T(8,128)} %bitcast.36), kind=kOutput, calls=%fused_computation.9 | convolution fusion | flops 6442450944 | bytes 25165824 | tf_op jit(solution)/shard_map/acfx,bcfx->afb/dot_general | solution.py:32
  214.4 0.0 copy-start.1
  214.4 34.0 %fusion.2 = f32[128,128,128]{2,1,0:T(8,128)} fusion(f32[128,1,128,128]{3,2,1,0:T(8,128)} %get-tuple-element.6, f32[128,1,128,128]{3,2,1,0:T(8,128)} %get-tuple-element.5), kind=kOutput, calls=%fused_computation.7 | convolution fusion | flops 3221225472 | bytes 25165824 | tf_op jit(solution)/shard_map/afx,bfx->afb/dot_general | solution.py:34
  248.3 0.0 copy-done.1
  248.4 30.0 %subtract_bitcast_fusion = f32[128,128,1,128]{0,3,1,2:T(8,128)} fusion(f32[128,128,128]{2,1,0:T(8,128)} %fusion.2, f32[128,1,128,128]{3,2,1,0:T(8,128)S(1)} %copy-done.1, f32[128,1,128,128]{3,2,1,0:T(8,128)} %get-tuple-element.6), kind=kOutput, calls=%fused_computation.6 | convolution fusion | flops 3223322624 | bytes 33554432 | tf_op jit(solution)/shard_map/afx,bfx->afb/dot_general | solution.py:33
  278.4 11.7 %pad_maximum_fusion = f32[128,128,2,128]{0,3,1,2:T(8,128)} fusion(f32[128,128,1,128]{0,3,1,2:T(8,128)} %subtract_bitcast_fusion, f32[128,128,1,128]{0,3,1,2:T(8,128)} %fusion.4), kind=kLoop, calls=%fused_computation | loop fusion | flops 4194304 | bytes 33554432 | tf_op jit(solution)/shard_map/stack | solution.py:37
  290.1 18.0 %copy.15 = f32[128,128,2,128]{3,1,2,0:T(8,128)} copy(f32[128,128,2,128]{0,3,1,2:T(8,128)} %pad_maximum_fusion) | data formatting | bytes 33554432 | tf_op jit(solution)/shard_map/stack | solution.py:37
  308.0 0.0 copy-start.2
  308.0 0.0 reduce-scatter.2.cloned.1.call-update
  308.0 0.0 all-reduce.3.cloned.1.call-start
  308.1 219.8 %reduce-scatter.2.cloned.1.call-done = f32[4,128,2,128]{3,1,2,0:T(8,128)} async-done(((f32[128,128,2,128]{3,1,2,0:T(8,128)}), f32[4,128,2,128]{3,1,2,0:T(8,128)}) %reduce-scatter.2.cloned.1.call-update) | async-done | bytes 524304 | tf_op jit(solution)/shard_map/reduce_scatter | solution.py:45
  527.9 2.2 copy.16
  530.1 0.0 all-reduce.3.cloned.1.call-update
  530.1 0.0 copy-done.2
  530.1 0.6 dynamic-slice
  531.4 76.4 %all-reduce.3.cloned.1.call-done = f32[4,128,2,128]{3,0,2,1:T(4,128)} async-done(((f32[4,128,2,128]{3,0,2,1:T(4,128)}), f32[4,128,2,128]{3,0,2,1:T(4,128)}) %all-reduce.3.cloned.1.call-update) | async-done | bytes 524304
  607.7 0.8 constant_dynamic-slice_fusion
  608.6 0.7 copy.17
  (1 shorter events, 0.0 us)
Async XLA Ops:
  19.1 120.3 %all-to-all-start = ((bf16[16,256,1024]{1,0,2:T(8,128)(2,1)}), bf16[16,256,1024]{1,0,2:T(8,128)(2,1)}, u32[]{:S(2)}, u32[]{:S(2)}) async-start(bf16[16,256,1024]{1,0,2:T(8,128)(2,1)} %copy.9), calls=%async_computation | async-start | bytes 16777216 | tf_op jit(solution)/shard_map/all_to_all | solution.py:41
  25.0 502.9 %reduce-scatter.2.cloned.1.call-start = ((), (), s32[]{:S(2)}) async-start(), calls=%async_computation.2 | async-start | bytes 17301504 | tf_op jit(solution)/shard_map/reduce_scatter | solution.py:45
  158.0 5.7 copy-start
  214.4 34.0 %copy-start.1 = (f32[128,1,128,128]{3,2,1,0:T(8,128)S(1)}, f32[128,1,128,128]{3,2,1,0:T(8,128)}, u32[]{:S(2)}) copy-start(f32[128,1,128,128]{3,2,1,0:T(8,128)} %get-tuple-element.5) | copy-start | bytes 25165828
  308.0 222.1 %copy-start.2 = (u32[256]{0:T(256)S(1)}, u32[256]{0:T(256)}, u32[]{:S(2)}) copy-start(u32[256]{0:T(256)} %constant.35) | copy-start | bytes 3076
  308.0 299.7 %all-reduce.3.cloned.1.call-start = ((), (), s32[]{:S(2)}) async-start(), calls=%async_computation.3 | async-start | bytes 1048576
Sparse Core Ops, SparseCore 0:
  308.2 219.6 reduce-scatter.1
  530.7 76.9 all-reduce.2
where the time goes:
time: 625 us; the launch traced here: 616 us
  waiting for transfers between devices  409 us (65%)
  matrix products  114 us (18%)
  local copies, waits for them, and re-layouts  60.4 us (10%)
  between operations  14.4 us (2%)
  other arithmetic  12.2 us (2%)
    reduce_scatter x1, waiting for transfers between devices, per_device(): lax.psum_scatter(cross_rows(coeffs), 'space', scatter_dimension=0, tiled=...  220 us
    all_to_all x1, waiting for transfers between devices, per_device(): lax.all_to_all(snapshots, 'tm', split_axis=2, concat_axis=0, tiled=True)  113 us
    unnamed x3, waiting for transfers between devices  76.4 us
    dot_general x1, matrix products, cross_rows(): real_part = jnp.einsum('acfx,bcfx->afb', coeffs, coeffs, precision=highest)  44.3 us
    dot_general x1, matrix products, cross_rows(): jnp.einsum('afx,bfx->afb', coeffs[:, 1], coeffs[:, 0], precision=highest)  34 us
    dot_general x1, matrix products, cross_rows(): jnp.einsum('afx,bfx->afb', coeffs[:, 0], coeffs[:, 1], precision=highest)  30 us
    unnamed x9, local copies, waits for them, and re-layouts  19.7 us
    another operation x1, local copies, waits for them, and re-layouts, cross_rows(): return jnp.stack([real_part, imag_part], axis=2)  18 us
  transfers between devices with their start and end apart: 3, of which 3 were waited for; matrix products, arithmetic and copies ran while one was open for 0% of the time, Pallas kernels for 0%

commit v1 on v0

v1 whole, which is shorter than its diff:
```python
import functools
import math

import jax
import jax.numpy as jnp
import ml_dtypes
import numpy as np
from jax import lax
from jax.experimental import pallas as pl
from jax.experimental.pallas import tpu as pltpu
from jax.sharding import PartitionSpec as P

CHUNKS = 1
LANES = 256


def table_rows(length, owners, chunks):
    count = length // 2
    steps_t = np.arange(length, dtype=np.int32)
    freqs = np.arange(count, dtype=np.int32)
    phase = (freqs[:, None] * steps_t[None, :] % length).astype(np.float32) * np.float32(
        2.0 * math.pi / length
    )
    hann = np.float32(0.5) - np.float32(0.5) * np.cos(
        steps_t.astype(np.float32) * np.float32(2.0 * math.pi / length)
    )
    factor = np.float32(1.0 / math.sqrt(3.0 * length / 8.0))
    table = np.stack([np.cos(phase), -np.sin(phase)], axis=1) * hann[None, None, :] * factor
    table = table.astype(ml_dtypes.bfloat16)
    per = count // owners // chunks
    table = table.reshape(owners, chunks, per, 2, length).transpose(1, 0, 2, 3, 4)
    return table.reshape(chunks, owners * per * 2, length)


def transform_kernel(table_ref, weights_ref, block_ref, out_ref, rows_ref):
    blocks = block_ref.shape[0]
    rows = table_ref.shape[0]
    lanes = block_ref.shape[2]
    scale = jnp.sqrt(weights_ref[...])
    for b in range(blocks):
        coeffs = jnp.dot(table_ref[...], block_ref[b], preferred_element_type=jnp.float32)
        coeffs = coeffs * scale
        for i in range(lanes // 128):
            rows_ref[i, pl.ds(b, rows, stride=blocks), :] = coeffs[:, i * 128 : (i + 1) * 128]
    for i in range(lanes // 128):
        ordered = rows_ref[i].astype(jnp.bfloat16)
        out_ref[:, :, i * 128 : (i + 1) * 128] = ordered.reshape(rows, blocks, 128)


def transform(table, weights, snapshots):
    blocks, length, points = snapshots.shape
    rows = table.shape[0]
    return pl.pallas_call(
        transform_kernel,
        grid=(points // LANES,),
        in_specs=[
            pl.BlockSpec((rows, length), lambda i: (0, 0)),
            pl.BlockSpec((1, LANES), lambda i: (0, i)),
            pl.BlockSpec((blocks, length, LANES), lambda i: (0, 0, i)),
        ],
        out_specs=pl.BlockSpec((rows, blocks, LANES), lambda i: (0, 0, i)),
        out_shape=jax.ShapeDtypeStruct((rows, blocks, points), jnp.bfloat16),
        scratch_shapes=[pltpu.VMEM((LANES // 128, rows * blocks, 128), jnp.float32)],
        compiler_params=pltpu.CompilerParams(vmem_limit_bytes=48 * 1024 * 1024),
        cost_estimate=pl.CostEstimate(
            flops=2 * rows * length * blocks * points,
            bytes_accessed=2 * blocks * points * (length + rows),
            transcendentals=0,
        ),
        name="transform",
    )(table, weights.reshape(1, points), snapshots)


def cross_kernel(coeffs_ref, out_ref):
    owners, _, blocks, points = coeffs_ref.shape
    spaces = out_ref.shape[0]
    total = owners * blocks
    mine = total // spaces
    real = coeffs_ref[:, 0].reshape(total, points)
    imag = coeffs_ref[:, 1].reshape(total, points)
    across = (((1,), (1,)), ((), ()))
    first = lax.dot_general(
        real, jnp.concatenate([real, imag], axis=0), across, preferred_element_type=jnp.float32
    )
    second = lax.dot_general(
        imag, jnp.concatenate([imag, real], axis=0), across, preferred_element_type=jnp.float32
    )
    real_part = first[:, :total] + second[:, :total]
    imag_part = first[:, total:] - second[:, total:]
    for s in range(spaces):
        out_ref[s, 0, :mine, :] = real_part[s * mine : (s + 1) * mine]
        out_ref[s, 0, mine:, :] = imag_part[s * mine : (s + 1) * mine]


def cross(coeffs, spaces):
    owners, rows, blocks, points = coeffs.shape
    total = owners * blocks
    freqs = rows // 2
    return pl.pallas_call(
        cross_kernel,
        grid=(freqs,),
        in_specs=[pl.BlockSpec((owners, 2, blocks, points), lambda k: (0, k, 0, 0))],
        out_specs=pl.BlockSpec((spaces, 1, 2 * total // spaces, total), lambda k: (0, k, 0, 0)),
        out_shape=jax.ShapeDtypeStruct((spaces, freqs, 2 * total // spaces, total), jnp.float32),
        compiler_params=pltpu.CompilerParams(vmem_limit_bytes=48 * 1024 * 1024),
        cost_estimate=pl.CostEstimate(
            flops=8 * freqs * total * total * points,
            bytes_accessed=2 * rows * total * points + 8 * freqs * total * total,
            transcendentals=0,
        ),
        name="cross",
    )(coeffs)


def per_device(owners, spaces, snapshots, weights):
    blocks, length, points = snapshots.shape
    tables = table_rows(length, owners, CHUNKS)
    parts = []
    for c in range(CHUNKS):
        coeffs = transform(jnp.asarray(tables[c]), weights, snapshots)
        coeffs = coeffs.reshape(owners, -1, blocks, points)
        moved = lax.all_to_all(coeffs, "tm", split_axis=0, concat_axis=0, tiled=True)
        rows = cross(moved, spaces)
        rows = lax.all_to_all(rows, "space", split_axis=0, concat_axis=0, tiled=True)
        parts.append(jnp.sum(rows, axis=0))
    spectra = jnp.concatenate(parts, axis=0)
    freqs, both, total = spectra.shape
    return spectra.reshape(freqs, 2, both // 2, total).transpose(2, 0, 1, 3)


def solution(mesh):
    placed = (P("tm", None, "space"), P("space"))
    return jax.shard_map(
        functools.partial(per_device, mesh.shape["tm"], mesh.shape["space"]),
        mesh=mesh,
        in_specs=placed,
        out_specs=P("space", "tm", None, None),
        check_vma=False,
    )
```

time: 625 us -> 191 us (0.31); the launches traced: 616 us -> 190 us
  waiting for transfers between devices: 409 us -> 0 us
  blocking collectives: 0 us -> 163 us
  matrix products: 114 us -> 0 us
  local copies, waits for them, and re-layouts: 60.4 us -> 2.29 us
  Pallas kernels: 0 us -> 24.5 us
  between operations: 14.4 us -> 0.02 us
  other arithmetic: 12.2 us -> 0.11 us
    reduce_scatter x1 -> x0, waiting for transfers between devices: 220 us -> none  [per_device(): lax.psum_scatter(cross_rows(coeffs), 'space', scatter_dimension=0, tiled=...]
    all_to_all x0 -> x2, blocking collectives: none -> 163 us  [the longest x1 97.5 us: per_device(): lax.all_to_all(coeffs, 'tm', split_axis=0, concat_axis=0, tiled=True)]
    dot_general x4 -> x0, matrix products: 114 us -> none  [the longest x1 44.3 us: cross_rows(): real_part = jnp.einsum('acfx,bcfx->afb', coeffs, coeffs, precision=highest)]
    all_to_all x1 -> x0, waiting for transfers between devices: 113 us -> none  [per_device(): lax.all_to_all(snapshots, 'tm', split_axis=2, concat_axis=0, tiled=True)]
    unnamed x3 -> x0, waiting for transfers between devices: 76.4 us -> none
    pallas_call x0 -> x2, Pallas kernels: none -> 24.5 us  [the longest x1 13 us: cross(): pl.pallas_call(cross_kernel, grid=(freqs,), in_specs=[pl.BlockSpec((owner...]
    unnamed x9 -> x4, local copies, waits for them, and re-layouts: 19.7 us -> 1.59 us
    another operation x1 -> x0, local copies, waits for them, and re-layouts: 18 us -> none  [cross_rows(): return jnp.stack([real_part, imag_part], axis=2)]
  transfers between devices with their start and end apart: 3 -> 0, of which waited for: 3 -> 0; matrix products, arithmetic and copies ran while one was open for 0% -> 0% of each run, Pallas kernels for 0% -> 0%
where the time goes in v1:
time: 191 us; the launch traced here: 190 us
  blocking collectives  163 us (85%)
  Pallas kernels  24.5 us (13%)
  local copies, waits for them, and re-layouts  2.29 us (1%)
    all_to_all x1, blocking collectives, per_device(): lax.all_to_all(coeffs, 'tm', split_axis=0, concat_axis=0, tiled=True)  97.5 us
    all_to_all x1, blocking collectives, per_device(): lax.all_to_all(rows, 'space', split_axis=0, concat_axis=0, tiled=True)  65.7 us
    pallas_call x1, Pallas kernels, cross(): pl.pallas_call(cross_kernel, grid=(freqs,), in_specs=[pl.BlockSpec((owner...  13 us
    pallas_call x1, Pallas kernels, transform(): pl.pallas_call(transform_kernel, grid=(points // LANES,), in_specs=[pl.Bl...  11.4 us

profile of v1, /device:TPU:1, one launch (start us, length us, event | category | flops | bytes accessed | tf_op | source)
XLA Modules:
  0.0 190.1 jit_solution(13130661149570594293)
XLA Ops:
  0.0 0.0 copy-start
  0.0 0.9 copy-done
  0.9 0.0 copy-start.1
  0.9 0.7 copy-done.1
  1.6 11.4 %transform.1 = bf16[256,16,1024]{2,1,0:T(8,128)(2,1)} custom-call(bf16[256,256]{1,0:T(8,128)(2,1)S(1)} %copy-done, f32[1,1024]{1,0:T(1,128)S(1)} %bitcast.5, bf16[16,256,1024]{2,1,0:T(8,128)(2,1)} %block_ref.1), custom_call_target="tpu_custom_call" | custom-call | flops 2147483648 | bytes 16777216 | tf_op jit(solution)/shard_map/transform/pallas_call | solution.py:53
  13.0 97.5 %all_to_all.10.coeffs_ref = bf16[8,32,16,1024]{3,2,1,0:T(8,128)(2,1)} all-to-all(bf16[8,32,16,1024]{3,2,1,0:T(8,128)(2,1)} %bitcast.6), channel_id=1, replica_groups=mesh['tm'=8,'space'=32] {'tm'}, dimensions={0} | all-to-all | bytes 16777216 | tf_op jit(solution)/shard_map/all_to_all | solution.py:122
  110.5 13.0 %cross.1 = f32[32,16,8,128]{3,2,1,0:T(8,128)S(1)} custom-call(bf16[8,32,16,1024]{3,2,1,0:T(8,128)(2,1)} %all_to_all.10.coeffs_ref), custom_call_target="tpu_custom_call" | custom-call | flops 2147483648 | bytes 10485760 | tf_op jit(solution)/shard_map/cross/pallas_call | solution.py:99
  123.6 65.7 %all_to_all.11 = f32[32,16,8,128]{3,2,1,0:T(8,128)S(1)} all-to-all(f32[32,16,8,128]{3,2,1,0:T(8,128)S(1)} %cross.1), channel_id=1, replica_groups=mesh['tm'=8,'space'=32] {'space'}, dimensions={0} | all-to-all | bytes 4194304 | tf_op jit(solution)/shard_map/all_to_all | solution.py:124
  189.2 0.1 reduce_sum.9
  189.4 0.7 copy.6
  (1 shorter events, 0.0 us)
Async XLA Ops:
  0.0 0.9 copy-start
  0.9 0.7 copy-start.1

commit v2 on v1

v2 whole, which is shorter than its diff:
```python
import functools
import math

import jax
import jax.numpy as jnp
import ml_dtypes
import numpy as np
from jax import lax
from jax.experimental import pallas as pl
from jax.experimental.pallas import tpu as pltpu
from jax.sharding import PartitionSpec as P

LANES = 512
PLANES = 2
MIB = 1024 * 1024


def make_table(length):
    count = length // 2
    steps_t = np.arange(length, dtype=np.int32)
    freqs = np.arange(count, dtype=np.int32)
    turn = np.float32(2.0 * math.pi / length)
    phase = (freqs[:, None] * steps_t[None, :] % length).astype(np.float32) * turn
    hann = np.float32(0.5) - np.float32(0.5) * np.cos(steps_t.astype(np.float32) * turn)
    factor = np.float32(1.0 / math.sqrt(3.0 * length / 8.0))
    table = np.stack([np.cos(phase), -np.sin(phase)], axis=1) * hann * factor
    return table.astype(ml_dtypes.bfloat16).reshape(2 * count, length)


def transform_kernel(table_ref, weights_ref, block_ref, out_ref, rows_ref):
    blocks = block_ref.shape[0]
    lanes = block_ref.shape[2]
    rows = table_ref.shape[0]
    stride = rows_ref.shape[1] // rows
    scale = jnp.sqrt(weights_ref[...])
    for b in range(blocks):
        coeffs = jnp.dot(table_ref[...], block_ref[b], preferred_element_type=jnp.float32)
        coeffs = coeffs * scale
        for i in range(lanes // 128):
            rows_ref[i, pl.ds(b, rows, stride=stride), :] = coeffs[:, i * 128 : (i + 1) * 128]
    for i in range(lanes // 128):
        for j in range(rows):
            ordered = rows_ref[i, j * stride : j * stride + blocks, :]
            out_ref[j, :, i * 128 : (i + 1) * 128] = ordered.astype(jnp.bfloat16)


def transform(table, weights, snapshots):
    blocks, length, points = snapshots.shape
    rows = table.shape[0]
    lanes = min(LANES, points)
    return pl.pallas_call(
        transform_kernel,
        grid=(points // lanes,),
        in_specs=[
            pl.BlockSpec((rows, length), lambda i: (0, 0)),
            pl.BlockSpec((1, lanes), lambda i: (0, i)),
            pl.BlockSpec((blocks, length, lanes), lambda i: (0, 0, i)),
        ],
        out_specs=pl.BlockSpec((rows, blocks, lanes), lambda i: (0, 0, i)),
        out_shape=jax.ShapeDtypeStruct((rows, blocks, points), jnp.bfloat16),
        scratch_shapes=[pltpu.VMEM((lanes // 128, rows * (blocks + 1), 128), jnp.float32)],
        compiler_params=pltpu.CompilerParams(vmem_limit_bytes=56 * MIB),
        cost_estimate=pl.CostEstimate(
            flops=2 * rows * length * blocks * points,
            bytes_accessed=2 * blocks * points * (length + rows),
            transcendentals=0,
        ),
        name="transform",
    )(table, weights.reshape(1, points), snapshots)


def cross_kernel(coeffs_ref, out_ref):
    owners, places, rows, blocks, points = coeffs_ref.shape
    spaces = out_ref.shape[0]
    total = owners * blocks
    mine = total // spaces
    for k in range(rows // 2):
        pieces = []
        for p in range(places):
            real = coeffs_ref[:, p, 2 * k].reshape(total, points)
            imag = coeffs_ref[:, p, 2 * k + 1].reshape(total, points)
            pieces.append(jnp.concatenate([real, imag], axis=0))
        both = jnp.concatenate(pieces, axis=1)
        grams = lax.dot_general(
            both, both, (((1,), (1,)), ((), ())), preferred_element_type=jnp.float32
        )
        real_part = grams[:total, :total] + grams[total:, total:]
        imag_part = grams[:total, total:] - grams[total:, :total]
        for s in range(spaces):
            out_ref[s, k, :mine, :] = real_part[s * mine : (s + 1) * mine]
            out_ref[s, k, mine:, :] = imag_part[s * mine : (s + 1) * mine]


def cross(coeffs, spaces):
    owners, places, rows, blocks, points = coeffs.shape
    total = owners * blocks
    freqs = rows // 2
    shape = (spaces, freqs, 2 * total // spaces, total)
    return pl.pallas_call(
        cross_kernel,
        in_specs=[pl.BlockSpec(memory_space=pltpu.VMEM)],
        out_specs=pl.BlockSpec(memory_space=pltpu.VMEM),
        out_shape=jax.ShapeDtypeStruct(shape, jnp.float32),
        compiler_params=pltpu.CompilerParams(vmem_limit_bytes=32 * MIB),
        cost_estimate=pl.CostEstimate(
            flops=8 * freqs * total * total * points * places,
            bytes_accessed=2 * rows * total * points * places + 8 * freqs * total * total,
            transcendentals=0,
        ),
        name="cross",
    )(coeffs)


def per_device(owners, spaces, snapshots, weights):
    blocks, length, points = snapshots.shape
    table = jnp.asarray(make_table(length))
    rest = spaces // 8
    places = PLANES * rest
    groups = [
        [t * spaces + z * rest + r for t in range(owners) for z in range(h, h + PLANES) for r in range(rest)]
        for h in range(0, spaces // rest, PLANES)
    ]
    coeffs = transform(table, weights, snapshots)
    coeffs = coeffs.reshape(owners * places, -1, blocks, points)
    moved = lax.all_to_all(
        coeffs, ("tm", "space"), split_axis=0, concat_axis=0, tiled=True, axis_index_groups=groups
    )
    sums = cross(moved.reshape(owners, places, -1, blocks, points), spaces)
    sums = lax.all_to_all(sums, "space", split_axis=0, concat_axis=0, tiled=True)
    freqs, both, total = sums.shape[1:]
    spectra = jnp.sum(sums.reshape(-1, places * freqs, both, total), axis=0)
    return spectra.reshape(places * freqs, 2, both // 2, total).transpose(2, 0, 1, 3)


def solution(mesh):
    placed = (P("tm", None, "space"), P("space"))
    return jax.shard_map(
        functools.partial(per_device, mesh.shape["tm"], mesh.shape["space"]),
        mesh=mesh,
        in_specs=placed,
        out_specs=P("space", "tm", None, None),
        check_vma=False,
    )
```

time: 191 us -> 140 us (0.73)
  blocking collectives: 163 us -> 128 us
  Pallas kernels: 24.5 us -> 10.6 us
    all_to_all x2, blocking collectives: 163 us -> 128 us  [the longest x1 107 us: per_device(): lax.all_to_all(coeffs, ('tm', 'space'), split_axis=0, concat_axis=0, tile...]
    pallas_call x2, Pallas kernels: 24.5 us -> 10.6 us  [the longest x1 8.26 us: transform(): pl.pallas_call(transform_kernel, grid=(points // lanes,), in_specs=[pl.Bl...]
where the time goes in v2:
time: 140 us; the launch traced here: 139 us
  blocking collectives  128 us (91%)
  Pallas kernels  10.6 us (8%)
    all_to_all x1, blocking collectives, per_device(): lax.all_to_all(coeffs, ('tm', 'space'), split_axis=0, concat_axis=0, tile...  107 us
    all_to_all x1, blocking collectives, per_device(): lax.all_to_all(sums, 'space', split_axis=0, concat_axis=0, tiled=True)  21 us
    pallas_call x1, Pallas kernels, transform(): pl.pallas_call(transform_kernel, grid=(points // lanes,), in_specs=[pl.Bl...  8.26 us

profile of v2, /device:TPU:1, one launch (start us, length us, event | category | flops | bytes accessed | tf_op | source)
XLA Modules:
  0.0 139.5 jit_solution(5926189372832146607)
XLA Ops:
  0.0 8.3 %transform.1 = bf16[256,16,1024]{2,1,0:T(8,128)(2,1)} custom-call(bf16[256,256]{1,0:T(8,128)(2,1)} %constant.4.clone.table_ref, f32[1,1024]{1,0:T(1,128)} %bitcast.13, bf16[16,256,1024]{2,1,0:T(8,128)(2,1)} %block_ref.1), custom_call_target="tpu_custom_call" | custom-call | flops 2147483648 | bytes 16777216 | tf_op jit(solution)/shard_map/transform/pallas_call | solution.py:51
  8.3 107.1 %all_to_all.10 = bf16[64,4,16,1024]{3,2,1,0:T(8,128)(2,1)S(1)} all-to-all(bf16[64,4,16,1024]{3,2,1,0:T(8,128)(2,1)} %bitcast.10), channel_id=1, replica_groups={{0,1,2,3,4,5,6,7,32,33,34,35,36,37,38,39,64,65,66,67,68,69,70,71,96,97,..., dimensions={0} | all-to-all | bytes 16777216 | tf_op jit(solution)/shard_map/all_to_all | solution.py:125
  115.4 2.4 %cross.1 = f32[32,2,8,128]{3,2,1,0:T(8,128)S(1)} custom-call(bf16[8,8,4,16,1024]{4,3,2,1,0:T(8,128)(2,1)S(1)} %bitcast.9), custom_call_target="tpu_custom_call" | custom-call | flops 2147483648 | bytes 8650752 | tf_op jit(solution)/shard_map/cross/pallas_call | solution.py:99
  117.7 21.0 %all_to_all.11 = f32[32,2,8,128]{3,2,1,0:T(8,128)S(1)} all-to-all(f32[32,2,8,128]{3,2,1,0:T(8,128)S(1)} %cross.1), channel_id=1, replica_groups=mesh['tm'=8,'space'=32] {'space'}, dimensions={0} | all-to-all | bytes 524288 | tf_op jit(solution)/shard_map/all_to_all | solution.py:129
  138.8 0.7 copy.6
  (2 shorter events, 0.0 us)

commit v3 on v2

v3 whole, which is shorter than its diff:
```python
import functools
import math

import jax
import jax.numpy as jnp
import numpy as np
from jax import lax
from jax.experimental import pallas as pl
from jax.experimental.pallas import tpu as pltpu
from jax.sharding import PartitionSpec as P

PARTS = 4
GROUPS = (2, 4, 4, 6)
AHEAD = 4
PLANES = 2
MIB = 1024 * 1024


def wave(steps, length):
    half = length // 2
    below = jnp.where(steps < half, steps, steps - half)
    angle = (half // 2 - below).astype(jnp.float32) * np.float32(2.0 * math.pi / length)
    square = angle * angle
    series = jnp.full_like(angle, np.float32(1.0 / math.factorial(13)))
    for n in (11, 9, 7, 5, 3, 1):
        sign = -1.0 if n % 4 == 3 else 1.0
        series = series * square + np.float32(sign / math.factorial(n))
    return jnp.where(steps < half, series * angle, -(series * angle))


def make_table(rows, length):
    row = lax.broadcasted_iota(jnp.int32, (rows, length), 0)
    step = lax.broadcasted_iota(jnp.int32, (rows, length), 1)
    turns = ((row >> 1) * step + (row & 1) * (length // 4)) & (length - 1)
    times = lax.broadcasted_iota(jnp.int32, (8, length), 1)
    hann = np.float32(0.5) - np.float32(0.5) * wave(times, length)
    factor = np.float32(1.0 / math.sqrt(3.0 * length / 8.0))
    table = wave(turns, length) * hann[:1] * factor
    return table.astype(jnp.bfloat16)


def transform_kernel(
    weights_ref, block_ref, out_ref, ready_ref, scale_ref, held_ref, rows_ref, sems
):
    blocks, length, points = block_ref.shape
    rows = ready_ref.shape[0]
    parts, tiles, spread, _ = rows_ref.shape
    stride = spread // rows
    lanes = points // parts
    second = pltpu.make_async_copy(weights_ref, scale_ref, sems.at[blocks])
    edges = np.cumsum((0,) + GROUPS)
    spans = [slice(int(a), int(b)) for a, b in zip(edges[:-1], edges[1:])]
    copies = [
        pltpu.make_async_copy(block_ref.at[span], held_ref.at[span], sems.at[g])
        for g, span in enumerate(spans)
    ]
    copies[0].start()
    second.start()
    for copy in copies[1:AHEAD]:
        copy.start()

    def reorder(h, start, stop):
        for j in range(start, stop):
            for i in range(tiles):
                ordered = rows_ref[h, i, j * stride : j * stride + blocks, :]
                lane = h * lanes + i * 128
                out_ref[j, :, lane : lane + 128] = ordered.astype(jnp.bfloat16)

    ready_ref[...] = make_table(rows, length)
    second.wait()
    scale_ref[...] = jnp.sqrt(scale_ref[...])

    def multiply(b, h):
        here = slice(h * lanes, (h + 1) * lanes)
        coeffs = jnp.dot(ready_ref[...], held_ref[b, :, here], preferred_element_type=jnp.float32)
        coeffs = coeffs * scale_ref[:, here]
        for i in range(tiles):
            rows_ref[h, i, pl.ds(b, rows, stride=stride), :] = coeffs[:, i * 128 : (i + 1) * 128]

    last = len(spans) - 1
    for g, span in enumerate(spans):
        copies[g].wait()
        if g + AHEAD <= last:
            copies[g + AHEAD].start()
        inside = range(span.start, span.stop)
        if g < last:
            for b in inside:
                for h in range(parts):
                    multiply(b, h)
        else:
            share = rows // len(inside)
            for h in range(parts):
                for n, b in enumerate(inside):
                    multiply(b, h)
                    if h > 0:
                        reorder(h - 1, n * share, (n + 1) * share if b + 1 < blocks else rows)
    reorder(parts - 1, 0, rows)


def transform(weights, snapshots):
    blocks, length, points = snapshots.shape
    rows = length
    tiles = points // PARTS // 128
    return pl.pallas_call(
        transform_kernel,
        in_specs=[pl.BlockSpec(memory_space=pl.ANY)] * 2,
        out_specs=pl.BlockSpec(memory_space=pltpu.VMEM),
        out_shape=jax.ShapeDtypeStruct((rows, blocks, points), jnp.bfloat16),
        scratch_shapes=[
            pltpu.VMEM((rows, length), jnp.bfloat16),
            pltpu.VMEM((1, points), jnp.float32),
            pltpu.VMEM((blocks, length, points), jnp.bfloat16),
            pltpu.VMEM((PARTS, tiles, rows * (blocks + 1), 128), jnp.float32),
            pltpu.SemaphoreType.DMA((blocks + 1,)),
        ],
        compiler_params=pltpu.CompilerParams(vmem_limit_bytes=40 * MIB),
        cost_estimate=pl.CostEstimate(
            flops=2 * rows * length * blocks * points,
            bytes_accessed=2 * blocks * points * (length + rows),
            transcendentals=0,
        ),
        name="transform",
    )(weights.reshape(1, points), snapshots)


def cross_kernel(coeffs_ref, out_ref):
    owners, places, rows, blocks, points = coeffs_ref.shape
    spaces = out_ref.shape[0]
    total = owners * blocks
    mine = total // spaces
    for k in range(rows // 2):
        pieces = []
        for p in range(places):
            real = coeffs_ref[:, p, 2 * k].reshape(total, points)
            imag = coeffs_ref[:, p, 2 * k + 1].reshape(total, points)
            pieces.append(jnp.concatenate([real, imag], axis=0))
        both = jnp.concatenate(pieces, axis=1)
        grams = lax.dot_general(
            both, both, (((1,), (1,)), ((), ())), preferred_element_type=jnp.float32
        )
        real_part = grams[:total, :total] + grams[total:, total:]
        imag_part = grams[:total, total:] - grams[total:, :total]
        for s in range(spaces):
            out_ref[s, k, :mine, :] = real_part[s * mine : (s + 1) * mine]
            out_ref[s, k, mine:, :] = imag_part[s * mine : (s + 1) * mine]


def cross(coeffs, spaces):
    owners, places, rows, blocks, points = coeffs.shape
    total = owners * blocks
    freqs = rows // 2
    shape = (spaces, freqs, 2 * total // spaces, total)
    return pl.pallas_call(
        cross_kernel,
        in_specs=[pl.BlockSpec(memory_space=pltpu.VMEM)],
        out_specs=pl.BlockSpec(memory_space=pltpu.VMEM),
        out_shape=jax.ShapeDtypeStruct(shape, jnp.float32),
        compiler_params=pltpu.CompilerParams(vmem_limit_bytes=32 * MIB),
        cost_estimate=pl.CostEstimate(
            flops=8 * freqs * total * total * points * places,
            bytes_accessed=2 * rows * total * points * places + 8 * freqs * total * total,
            transcendentals=0,
        ),
        name="cross",
    )(coeffs)


def per_device(owners, spaces, snapshots, weights):
    blocks, _, points = snapshots.shape
    rest = spaces // 8
    places = PLANES * rest
    groups = [
        [t * spaces + z * rest + r for t in range(owners) for z in range(h, h + PLANES) for r in range(rest)]
        for h in range(0, spaces // rest, PLANES)
    ]
    coeffs = transform(weights, snapshots)
    coeffs = coeffs.reshape(owners * places, -1, blocks, points)
    moved = lax.all_to_all(
        coeffs, ("tm", "space"), split_axis=0, concat_axis=0, tiled=True, axis_index_groups=groups
    )
    sums = cross(moved.reshape(owners, places, -1, blocks, points), spaces)
    sums = lax.all_to_all(sums, "space", split_axis=0, concat_axis=0, tiled=True)
    freqs, both, total = sums.shape[1:]
    spectra = jnp.sum(sums.reshape(-1, places * freqs, both, total), axis=0)
    return spectra.reshape(places * freqs, 2, both // 2, total).transpose(2, 0, 1, 3)


def solution(mesh):
    placed = (P("tm", None, "space"), P("space"))
    return jax.shard_map(
        functools.partial(per_device, mesh.shape["tm"], mesh.shape["space"]),
        mesh=mesh,
        in_specs=placed,
        out_specs=P("space", "tm", None, None),
        check_vma=False,
    )
```

time: 140 us -> 138 us (0.986)
  Pallas kernels: 10.6 us -> 8.39 us
    pallas_call x1, Pallas kernels: 8.26 us -> 6.04 us  [transform(): pl.pallas_call(transform_kernel, in_specs=[pl.BlockSpec(memory_space=pl.A...]
where the time goes in v3:
time: 138 us
  blocking collectives  128 us (93%)
  Pallas kernels  8.39 us (6%)
    all_to_all x1, blocking collectives, per_device(): lax.all_to_all(coeffs, ('tm', 'space'), split_axis=0, concat_axis=0, tile...  107 us
    all_to_all x1, blocking collectives, per_device(): lax.all_to_all(sums, 'space', split_axis=0, concat_axis=0, tiled=True)  21 us
    pallas_call x1, Pallas kernels, transform(): pl.pallas_call(transform_kernel, in_specs=[pl.BlockSpec(memory_space=pl.A...  6.04 us

profile of v3, /device:TPU:1, one launch (start us, length us, event | category | flops | bytes accessed | tf_op | source)
XLA Modules:
  0.0 137.8 jit_solution(15517333185978527538)
XLA Ops:
  0.0 0.0 copy-start
  0.0 0.7 copy-done
  0.7 6.0 %transform.1 = bf16[256,16,1024]{2,1,0:T(8,128)(2,1)S(1)} custom-call(f32[1,1024]{1,0:T(1,128)S(1)} %bitcast.11, bf16[16,256,1024]{2,1,0:T(8,128)(2,1)} %block_ref.1), custom_call_target="tpu_custom_call" | custom-call | flops 2147483648 | bytes 16777216 | tf_op jit(solution)/shard_map/transform/pallas_call | solution.py:104
  6.7 106.9 %all_to_all.10 = bf16[64,4,16,1024]{3,2,1,0:T(8,128)(2,1)S(1)} all-to-all(bf16[64,4,16,1024]{3,2,1,0:T(8,128)(2,1)S(1)} %bitcast.9), channel_id=1, replica_groups={{0,1,2,3,4,5,6,7,32,33,34,35,36,37,38,39,64,65,66,67,68,69,70,71,96,97,..., dimensions={0} | all-to-all | bytes 16777216 | tf_op jit(solution)/shard_map/all_to_all | solution.py:178
  113.7 2.4 %cross.1 = f32[32,2,8,128]{3,2,1,0:T(8,128)S(1)} custom-call(bf16[8,8,4,16,1024]{4,3,2,1,0:T(8,128)(2,1)S(1)} %bitcast.10), custom_call_target="tpu_custom_call" | custom-call | flops 2147483648 | bytes 8650752 | tf_op jit(solution)/shard_map/cross/pallas_call | solution.py:153
  116.0 21.0 %all_to_all.11 = f32[32,2,8,128]{3,2,1,0:T(8,128)S(1)} all-to-all(f32[32,2,8,128]{3,2,1,0:T(8,128)S(1)} %cross.1), channel_id=1, replica_groups=mesh['tm'=8,'space'=32] {'space'}, dimensions={0} | all-to-all | bytes 524288 | tf_op jit(solution)/shard_map/all_to_all | solution.py:182
  137.1 0.7 copy.5
  (2 shorter events, 0.0 us)
Async XLA Ops:
  0.0 0.7 copy-start

commit v4 on v3

--- a/solution.py
+++ b/solution.py
@@ -165,6 +165,28 @@
     )(coeffs)
 
 
+def gather_kernel(sums_ref, out_ref):
+    total = sums_ref[0]
+    for n in range(1, sums_ref.shape[0]):
+        total = total + sums_ref[n]
+    mine = out_ref.shape[0]
+    for a in range(mine):
+        for part in range(2):
+            out_ref[a, :, part, :] = total[:, part * mine + a, :]
+
+
+def gather(sums):
+    _, freqs, both, total = sums.shape
+    return pl.pallas_call(
+        gather_kernel,
+        in_specs=[pl.BlockSpec(memory_space=pltpu.VMEM)],
+        out_specs=pl.BlockSpec(memory_space=pltpu.VMEM),
+        out_shape=jax.ShapeDtypeStruct((both // 2, freqs, 2, total), jnp.float32),
+        compiler_params=pltpu.CompilerParams(vmem_limit_bytes=8 * MIB),
+        name="gather",
+    )(sums)
+
+
 def per_device(owners, spaces, snapshots, weights):
     blocks, _, points = snapshots.shape
     rest = spaces // 8
@@ -181,8 +203,7 @@
     sums = cross(moved.reshape(owners, places, -1, blocks, points), spaces)
     sums = lax.all_to_all(sums, "space", split_axis=0, concat_axis=0, tiled=True)
     freqs, both, total = sums.shape[1:]
-    spectra = jnp.sum(sums.reshape(-1, places * freqs, both, total), axis=0)
-    return spectra.reshape(places * freqs, 2, both // 2, total).transpose(2, 0, 1, 3)
+    return gather(sums.reshape(-1, places * freqs, both, total))
 
 
 def solution(mesh):

time: 138 us -> 138 us (level)
  no operation moved by 1% of the time
where the time goes in v4:
time: 138 us
  blocking collectives  128 us (93%)
  Pallas kernels  9.05 us (7%)
    all_to_all x1, blocking collectives, per_device(): lax.all_to_all(coeffs, ('tm', 'space'), split_axis=0, concat_axis=0, tile...  107 us
    all_to_all x1, blocking collectives, per_device(): lax.all_to_all(sums, 'space', split_axis=0, concat_axis=0, tiled=True)  21 us
    pallas_call x1, Pallas kernels, transform(): pl.pallas_call(transform_kernel, in_specs=[pl.BlockSpec(memory_space=pl.A...  6.04 us

profile of v4, /device:TPU:1, one launch (start us, length us, event | category | flops | bytes accessed | tf_op | source)
XLA Modules:
  0.0 137.7 jit_solution(5384729149825037373)
XLA Ops:
  0.0 0.0 copy-start
  0.0 0.7 copy-done
  0.7 6.0 %transform.1 = bf16[256,16,1024]{2,1,0:T(8,128)(2,1)S(1)} custom-call(f32[1,1024]{1,0:T(1,128)S(1)} %bitcast.7, bf16[16,256,1024]{2,1,0:T(8,128)(2,1)} %block_ref.1), custom_call_target="tpu_custom_call" | custom-call | flops 2147483648 | bytes 16777216 | tf_op jit(solution)/shard_map/transform/pallas_call | solution.py:104
  6.7 106.9 %all_to_all.10 = bf16[64,4,16,1024]{3,2,1,0:T(8,128)(2,1)S(1)} all-to-all(bf16[64,4,16,1024]{3,2,1,0:T(8,128)(2,1)S(1)} %bitcast.4), channel_id=1, replica_groups={{0,1,2,3,4,5,6,7,32,33,34,35,36,37,38,39,64,65,66,67,68,69,70,71,96,97,..., dimensions={0} | all-to-all | bytes 16777216 | tf_op jit(solution)/shard_map/all_to_all | solution.py:200
  113.7 2.4 %cross.1 = f32[32,2,8,128]{3,2,1,0:T(8,128)S(1)} custom-call(bf16[8,8,4,16,1024]{4,3,2,1,0:T(8,128)(2,1)S(1)} %bitcast.5), custom_call_target="tpu_custom_call" | custom-call | flops 2147483648 | bytes 8650752 | tf_op jit(solution)/shard_map/cross/pallas_call | solution.py:153
  116.0 21.0 %all_to_all.11 = f32[32,2,8,128]{3,2,1,0:T(8,128)S(1)} all-to-all(f32[32,2,8,128]{3,2,1,0:T(8,128)S(1)} %cross.1), channel_id=1, replica_groups=mesh['tm'=8,'space'=32] {'space'}, dimensions={0} | all-to-all | bytes 524288 | tf_op jit(solution)/shard_map/all_to_all | solution.py:204
  137.0 0.7 gather.1
Async XLA Ops:
  0.0 0.7 copy-start

commit v5 on v4

--- a/solution.py
+++ b/solution.py
@@ -10,8 +10,8 @@
 from jax.sharding import PartitionSpec as P
 
 PARTS = 4
-GROUPS = (2, 4, 4, 6)
-AHEAD = 4
+GROUPS = (1, 2, 3, 4, 6)
+AHEAD = 5
 PLANES = 2
 MIB = 1024 * 1024
 

time: 138 us -> 138 us (level)
  no operation moved by 1% of the time
where the time goes in v5:
time: 138 us
  blocking collectives  128 us (93%)
  Pallas kernels  9.06 us (7%)
    all_to_all x1, blocking collectives, per_device(): lax.all_to_all(coeffs, ('tm', 'space'), split_axis=0, concat_axis=0, tile...  107 us
    all_to_all x1, blocking collectives, per_device(): lax.all_to_all(sums, 'space', split_axis=0, concat_axis=0, tiled=True)  21 us
    pallas_call x1, Pallas kernels, transform(): pl.pallas_call(transform_kernel, in_specs=[pl.BlockSpec(memory_space=pl.A...  6.05 us

profile of v5, /device:TPU:1, one launch (start us, length us, event | category | flops | bytes accessed | tf_op | source)
XLA Modules:
  0.0 137.7 jit_solution(9132997878923724278)
XLA Ops:
  0.0 0.0 copy-start
  0.0 0.7 copy-done
  0.7 6.0 %transform.1 = bf16[256,16,1024]{2,1,0:T(8,128)(2,1)S(1)} custom-call(f32[1,1024]{1,0:T(1,128)S(1)} %bitcast.7, bf16[16,256,1024]{2,1,0:T(8,128)(2,1)} %block_ref.1), custom_call_target="tpu_custom_call" | custom-call | flops 2147483648 | bytes 16777216 | tf_op jit(solution)/shard_map/transform/pallas_call | solution.py:104
  6.7 106.9 %all_to_all.10 = bf16[64,4,16,1024]{3,2,1,0:T(8,128)(2,1)S(1)} all-to-all(bf16[64,4,16,1024]{3,2,1,0:T(8,128)(2,1)S(1)} %bitcast.4), channel_id=1, replica_groups={{0,1,2,3,4,5,6,7,32,33,34,35,36,37,38,39,64,65,66,67,68,69,70,71,96,97,..., dimensions={0} | all-to-all | bytes 16777216 | tf_op jit(solution)/shard_map/all_to_all | solution.py:200
  113.6 2.4 %cross.1 = f32[32,2,8,128]{3,2,1,0:T(8,128)S(1)} custom-call(bf16[8,8,4,16,1024]{4,3,2,1,0:T(8,128)(2,1)S(1)} %bitcast.5), custom_call_target="tpu_custom_call" | custom-call | flops 2147483648 | bytes 8650752 | tf_op jit(solution)/shard_map/cross/pallas_call | solution.py:153
  116.0 21.0 %all_to_all.11 = f32[32,2,8,128]{3,2,1,0:T(8,128)S(1)} all-to-all(f32[32,2,8,128]{3,2,1,0:T(8,128)S(1)} %cross.1), channel_id=1, replica_groups=mesh['tm'=8,'space'=32] {'space'}, dimensions={0} | all-to-all | bytes 524288 | tf_op jit(solution)/shard_map/all_to_all | solution.py:204
  137.1 0.7 gather.1
Async XLA Ops:
  0.0 0.7 copy-start
